TPU v7x, 256 devices: a whole 4x4x8 slice. The times are simulated.
256 devices in a mesh: dp: 4 (over y), height: 8 (over z_hi, x), tensor: 8 (over z_lo, core).
Axes of the slice: x: 4, y: 4, z: 8 (z_hi: 2, z_lo: 4; z = z_hi * 4 + z_lo), core: 2. Of those that a mesh axis runs over, the one named last changes fastest.
Arguments:
- features: bfloat16 [4, 4, 16, 32, 512], P('dp', None, 'height', None, 'tensor'), may hold values from -6 to 6
- cotangent: bfloat16 [4, 4, 16, 32, 512], P('dp', None, 'height', None, 'tensor'), may hold values from -6 to 6
- conv_one: bfloat16 [27, 512, 512], P(None, 'tensor'), may hold values from -0.0546875 to 0.0546875
- bias_one: float32 [512], P('tensor'), may hold values from -4 to 4
- conv_two: bfloat16 [27, 512, 512], P(None, 'tensor'), may hold values from -0.0546875 to 0.0546875
Outputs:
- grad_features: bfloat16 [4, 4, 16, 32, 512], P('dp', None, 'height', None, 'tensor')
- grad_one: float32 [27, 512, 512], P(None, ('dp', 'height'), 'tensor')
- grad_two: float32 [27, 512, 512], P(None, ('dp', 'height'), 'tensor')
All inputs are finite; a program needn't handle non-finite values.
Results may differ from a plain program's by a relative error of at most 0.0052.
Values may be sent and summed in bfloat16 or wider, within the bound.
A program may use at most 128 MiB of HBM per device.

v0:
```python
import math

import jax
import jax.numpy as jnp
from jax import lax
from jax.sharding import PartitionSpec as P


def with_halo(array, sides, width):
    for axis, dim in sides:
        peers, length = (lax.axis_size(axis), array.shape[dim])
        up = [(i, (i + 1) % peers) for i in range(peers - 1)]
        down = [(j, i) for i, j in up]
        last = lax.slice_in_dim(array, length - width, length, axis=dim)
        initial = lax.slice_in_dim(array, 0, width, axis=dim)
        before = lax.ppermute(last, axis, up)
        after = lax.ppermute(initial, axis, down)
        array = jnp.concatenate([before, array, after], axis=dim)
    return array


def silu_slope(value):
    sig = jax.nn.sigmoid(value)
    return sig * (1.0 + value * (1.0 - sig))


def forward_patches(extended, frames, row_count, col_count):
    padded = jnp.pad(extended, ((0, 0), (2, 0), (0, 0), (1, 1), (0, 0)))
    windows = [
        padded[
            :,
            shift_time : shift_time + frames,
            shift_row : shift_row + row_count,
            shift_col : shift_col + col_count,
            :,
        ]
        for shift_time in range(3)
        for shift_row in range(3)
        for shift_col in range(3)
    ]
    stacked = jnp.stack(windows, axis=-2)
    return stacked.reshape(-1, stacked.shape[-2] * stacked.shape[-1])


def backward_patches(extended, frames, row_count, col_count):
    padded = jnp.pad(extended, ((0, 0), (0, 2), (0, 0), (1, 1), (0, 0)))
    windows = [
        padded[
            :,
            2 - shift_time : 2 - shift_time + frames,
            2 - shift_row : 2 - shift_row + row_count,
            2 - shift_col : 2 - shift_col + col_count,
            :,
        ]
        for shift_time in range(3)
        for shift_row in range(3)
        for shift_col in range(3)
    ]
    stacked = jnp.stack(windows, axis=-2)
    return stacked.reshape(-1, stacked.shape[-2] * stacked.shape[-1])


def contract_rows(left, right):
    return lax.dot_general(
        left, right, (((0,), (0,)), ((), ())), preferred_element_type=jnp.float32
    )


def apply_kernel(patches, kernel):
    shaped = patches.reshape(patches.shape[0], kernel.shape[0], kernel.shape[2])
    return lax.dot_general(
        shaped, kernel, (((1, 2), (0, 2)), ((), ())), preferred_element_type=jnp.float32
    )


def widen(value):
    return lax.all_gather(value, "tensor", axis=4, tiled=True)


def with_rims(value):
    return with_halo(value, (("height", 2),), 1)


def settle(partial_sum):
    return lax.psum_scatter(partial_sum, "tensor", scatter_dimension=4, tiled=True)


def settle_grads(terms):
    return (
        lax.psum_scatter(terms[0], ("dp", "height"), scatter_dimension=1, tiled=True),
        lax.psum_scatter(terms[1], ("dp", "height"), scatter_dimension=1, tiled=True),
    )


def local(features, cotangent, conv_one, bias_one, conv_two):
    clips_here, frames, row_count, col_count, narrow = features.shape
    channels = conv_one.shape[2]
    shape_local = features.shape
    shape_wide = (clips_here, frames, row_count, col_count, channels)
    grad_scale = 1.0 / math.sqrt(
        clips_here * lax.axis_size("dp") * frames * row_count * lax.axis_size("height") * col_count
    )
    feat_float = features.astype(jnp.float32)
    act_one = jax.nn.silu(feat_float).astype(jnp.bfloat16)
    patch_one = forward_patches(with_rims(widen(act_one)), frames, row_count, col_count)
    preact = apply_kernel(patch_one, conv_one).reshape(shape_local) + bias_one
    act_two = jax.nn.silu(preact).astype(jnp.bfloat16)
    patch_two = forward_patches(with_rims(widen(act_two)), frames, row_count, col_count)
    grad_two = (
        contract_rows(patch_two, cotangent.reshape(-1, narrow)).reshape(27, channels, narrow)
        * grad_scale
    )
    flip_two = conv_two.reshape(-1, channels)
    part_two = jnp.dot(
        backward_patches(with_rims(cotangent), frames, row_count, col_count),
        flip_two,
        preferred_element_type=jnp.float32,
    ).reshape(shape_wide)
    back_two = settle(part_two)
    grad_pre = (back_two * silu_slope(preact)).astype(jnp.bfloat16)
    grad_one = (
        contract_rows(patch_one, grad_pre.reshape(-1, narrow)).reshape(27, channels, narrow)
        * grad_scale
    )
    flip_one = conv_one.reshape(-1, channels)
    part_one = jnp.dot(
        backward_patches(with_rims(grad_pre), frames, row_count, col_count),
        flip_one,
        preferred_element_type=jnp.float32,
    ).reshape(shape_wide)
    back_one = settle(part_one)
    grad_in = (cotangent.astype(jnp.float32) + back_one * silu_slope(feat_float)).astype(
        jnp.bfloat16
    )
    grad_two, grad_one = settle_grads((grad_two, grad_one))
    return (grad_in, grad_one, grad_two)


def solution(mesh):
    in_specs = (
        P("dp", None, "height", None, "tensor"),
        P("dp", None, "height", None, "tensor"),
        P(None, "tensor", None),
        P("tensor"),
        P(None, "tensor", None),
    )
    out_specs = (
        P("dp", None, "height", None, "tensor"),
        P(None, ("dp", "height"), "tensor"),
        P(None, ("dp", "height"), "tensor"),
    )
    return jax.shard_map(local, mesh=mesh, in_specs=in_specs, out_specs=out_specs, check_vma=False)
```

profile of v0, /device:TPU:2, one launch (start us, length us, event | category | flops | bytes accessed | tf_op | source)
XLA Modules:
  0.0 743.2 jit_solution(8721555420672601654)
XLA Ops:
  8.1 3.4 collective-permute-start
  11.5 2.4 collective-permute-start.1
  15.0 18.7 %all_gather.6 = bf16[1,4,2,32,512]{3,1,2,0,4:T(4,128)(2,1)} all-gather(bf16[1,4,2,32,64]{3,1,2,0,4:T(4,128)(2,1)S(1)} %copy.296), channel_id=1, replica_groups=mesh['dp'=4,'height'=8,'tensor'=8] {'tensor'}, dimensions={4}, use_global_device_ids=true | all-gather | bytes 294912 | tf_op jit(solution)/shard_map/all_gather | solution.py:77
  33.7 1.5 copy.297
  35.9 3.4 collective-permute-start.2
  39.3 2.4 collective-permute-start.3
  45.1 2.5 copy.295
  47.6 3.2 reshape.171
  50.8 2.9 convolution_bitcast_fusion.1
  53.8 3.9 copy.345
  57.6 4.4 reshape.187
  103.3 6.3 reduce-scatter.13.cloned.1.call-done
  110.8 5.0 fusion.83
  115.9 3.4 collective-permute-start.4
  119.3 2.9 collective-permute-start.5
  123.1 10.9 %copy.330 = bf16[1,4,2,32,27,512]{5,4,3,2,1,0:T(8,128)(2,1)} copy(bf16[1,4,2,32,27,512]{5,3,2,1,4,0:T(8,128)(2,1)} %constant_dynamic-update-slice_fusion.81) | data formatting | bytes 14155776 | tf_op jit(solution)/shard_map/stack | solution.py:41
  134.0 13.9 %copy.349 = bf16[32,8,27,512]{3,1,2,0:T(8,128)(2,1)} copy(bf16[32,8,27,512]{3,2,1,0:T(8,128)(2,1)} %bitcast.549) | data formatting | bytes 14155776
  147.9 10.3 %copy.331 = bf16[13824,256]{1,0:T(8,128)(2,1)} copy(bf16[13824,256]{0,1:T(8,128)(2,1)} %bitcast.551) | data formatting | bytes 14155776 | tf_op jit(solution)/shard_map/dot_general | solution.py:64
  159.0 2.6 copy.328
  161.6 3.2 reshape.173
  164.8 1.4 convolution_bitcast_fusion
  166.2 3.9 copy.347
  170.1 4.4 reshape.189
  174.8 16.4 %all-gather = bf16[4,2,32,512]{2,0,1,3:T(4,128)(2,1)S(1)} all-gather(bf16[4,2,32,64]{2,0,1,3:T(4,128)(2,1)S(1)} %copy.333), channel_id=2, replica_groups=mesh['dp'=4,'height'=8,'tensor'=8] {'tensor'}, dimensions={3}, use_global_device_ids=true | all-gather | bytes 294912 | tf_op jit(solution)/shard_map/all_gather | solution.py:77
  191.2 1.3 fusion.88
  192.6 6.1 collective-permute-start.6
  198.7 1.9 collective-permute-start.7
  200.6 7.9 %broadcast_multiply_fusion.1 = f32[27,512,64]{2,1,0:T(8,128)} fusion(bf16[27,512,256]{2,1,0:T(8,128)(2,1)} %bitcast.543, bf16[256,64,1]{1,0,2:T(8,128)(2,1)S(1)} %bitcast.556), kind=kOutput, calls=%fused_computation.14 | convolution fusion | flops 453869568 | bytes 10649600 | tf_op jit(solution)/shard_map/dot_general | solution.py:64
  208.6 2.0 collective-permute-done.6
  210.6 10.1 %collective-permute-done.7 = bf16[1,4,1,32,512]{3,1,2,4,0:T(4,128)(2,1)S(1)} collective-permute-done((bf16[1,4,1,32,512]{3,1,2,4,0:T(4,128)(2,1)}, bf16[1,4,1,32,512]{3,1,2,4,0:T(4,128)(2,1)S(1)}, u32[]{:S(2)}, u32[]{:S(2)}) %collective-permute-start.7) | collective-permute-done | bytes 131104 | tf_op jit(solution)/shard_map/ppermute | solution.py:17
  220.7 4.5 fusion.7
  225.2 1.3 fusion.50
  226.6 1.6 fusion.49
  228.2 1.6 fusion.48
  229.8 1.4 fusion.47
  231.2 1.6 fusion.46
  232.8 1.6 fusion.45
  234.4 1.3 fusion.44
  235.8 1.7 fusion.43
  237.4 1.7 fusion.42
  239.1 1.5 fusion.41
  240.6 1.8 fusion.40
  242.5 1.9 fusion.39
  244.3 1.6 fusion.38
  245.9 1.8 fusion.37
  247.7 1.8 fusion.36
  249.6 1.5 fusion.35
  251.1 1.8 fusion.34
  252.9 2.3 fusion.33
  255.2 1.5 fusion.32
  256.7 1.5 fusion.31
  258.3 1.8 fusion.29
  260.1 1.6 fusion.28
  261.6 1.3 bitcast_dynamic-update-slice_fusion
  263.0 1.9 fusion.27
  264.9 1.6 fusion.26
  266.5 1.7 fusion.25
  268.1 1.8 fusion.23
  270.0 33.7 %copy.334 = bf16[1,4,2,32,27,512]{5,4,3,2,1,0:T(8,128)(2,1)} copy(bf16[1,4,2,32,27,512]{3,1,2,5,4,0:T(4,128)(2,1)} %fusion.23) | data formatting | bytes 14155776 | tf_op jit(solution)/shard_map/stack | solution.py:41
  303.7 13.7 %copy.350 = bf16[32,8,27,512]{3,1,2,0:T(8,128)(2,1)} copy(bf16[32,8,27,512]{3,2,1,0:T(8,128)(2,1)} %bitcast.550) | data formatting | bytes 14155776
  317.4 10.3 %copy.335 = bf16[13824,256]{1,0:T(8,128)(2,1)} copy(bf16[13824,256]{0,1:T(8,128)(2,1)} %bitcast.552) | data formatting | bytes 14155776 | tf_op jit(solution)/shard_map/dot_general | solution.py:64
  327.7 8.0 %broadcast_multiply_fusion = f32[27,512,64]{2,1,0:T(8,128)} fusion(bf16[27,512,256]{2,1,0:T(8,128)(2,1)} %bitcast.544, bf16[256,64,1]{1,0,2:T(8,128)(2,1)S(1)} %bitcast.555), kind=kOutput, calls=%fused_computation.13 | convolution fusion | flops 453869568 | bytes 10649600 | tf_op jit(solution)/shard_map/dot_general | solution.py:64
  337.7 138.4 %reduce-scatter.9.cloned.1.call-done = f32[27,16,64]{2,1,0:T(8,128)} async-done(((f32[27,512,64]{2,1,0:T(8,128)}), f32[27,16,64]{2,1,0:T(8,128)}) %reduce-scatter.9.cloned.1.call-update) | async-done | bytes 110608 | tf_op jit(solution)/shard_map/reduce_scatter | solution.py:91
  476.1 260.4 %reduce-scatter.11.cloned.1.call-done = f32[27,16,64]{2,1,0:T(8,128)} async-done(((f32[27,512,64]{2,1,0:T(8,128)}), f32[27,16,64]{2,1,0:T(8,128)}) %reduce-scatter.11.cloned.1.call-update) | async-done | bytes 110608 | tf_op jit(solution)/shard_map/reduce_scatter | solution.py:90
  (148 shorter events, 52.0 us)
Async XLA Ops:
  7.2 103.7 %copy-start = (bf16[27,64,512]{2,1,0:T(8,128)(2,1)S(1)}, bf16[27,64,512]{2,1,0:T(8,128)(2,1)}, u32[]{:S(2)}) copy-start(bf16[27,64,512]{2,1,0:T(8,128)(2,1)} %param.7) | copy-start | bytes 5308420
  7.2 37.8 %copy-start.2 = (bf16[1,4,2,32,64]{4,3,2,1,0:T(8,128)(2,1)S(1)}, bf16[1,4,2,32,64]{4,3,2,1,0:T(8,128)(2,1)}, u32[]{:S(2)}) copy-start(bf16[1,4,2,32,64]{4,3,2,1,0:T(8,128)(2,1)} %param.6) | copy-start | bytes 98308
  7.2 102.4 %reduce-scatter.13.cloned.1.call-start = ((), (), s32[]{:S(2)}) async-start(), calls=%async_computation.6 | async-start | bytes 589824
  8.1 33.6 %collective-permute-start = (bf16[1,4,1,32,64]{4,3,2,1,0:T(8,128)(2,1)S(1)}, bf16[1,4,1,32,64]{4,3,2,1,0:T(8,128)(2,1)S(1)}, u32[]{:S(2)}, u32[]{:S(2)}) collective-permute-start(bf16[1,4,1,32,64]{4,3,2,1,0:T(8,128)(2,1)S(1)} %get-tuple-element.21), channel_id=1, source_target_pairs={{0,8},{8,16},{16,24},{24,32},{32,40},{40,48},{48,56},{1,9},{9,17},... | collective-permute-start | bytes 49160 | tf_op jit(solution)/shard_map/ppermute | solution.py:16
  11.5 30.2 %collective-permute-start.1 = (bf16[1,4,1,32,64]{4,3,2,1,0:T(8,128)(2,1)S(1)}, bf16[1,4,1,32,64]{4,3,2,1,0:T(8,128)(2,1)S(1)}, u32[]{:S(2)}, u32[]{:S(2)}) collective-permute-start(bf16[1,4,1,32,64]{4,3,2,1,0:T(8,128)(2,1)S(1)} %get-tuple-element.22), channel_id=1, source_target_pairs={{8,0},{16,8},{24,16},{32,24},{40,32},{48,40},{56,48},{9,1},{17,9},... | collective-permute-start | bytes 49160 | tf_op jit(solution)/shard_map/ppermute | solution.py:17
  35.9 26.5 %collective-permute-start.2 = (bf16[1,4,1,32,512]{4,3,2,1,0:T(8,128)(2,1)}, bf16[1,4,1,32,512]{4,3,2,1,0:T(8,128)(2,1)S(1)}, u32[]{:S(2)}, u32[]{:S(2)}) collective-permute-start(bf16[1,4,1,32,512]{4,3,2,1,0:T(8,128)(2,1)} %get-tuple-element.17), channel_id=1, source_target_pairs={{0,8},{8,16},{16,24},{24,32},{32,40},{40,48},{48,56},{1,9},{9,17},... | collective-permute-start | bytes 393224 | tf_op jit(solution)/shard_map/ppermute | solution.py:16
  39.3 23.1 %collective-permute-start.3 = (bf16[1,4,1,32,512]{4,3,2,1,0:T(8,128)(2,1)S(1)}, bf16[1,4,1,32,512]{4,3,2,1,0:T(8,128)(2,1)S(1)}, u32[]{:S(2)}, u32[]{:S(2)}) collective-permute-start(bf16[1,4,1,32,512]{4,3,2,1,0:T(8,128)(2,1)S(1)} %get-tuple-element.18), channel_id=1, source_target_pairs={{8,0},{16,8},{24,16},{32,24},{40,32},{48,40},{56,48},{9,1},{17,9},... | collective-permute-start | bytes 393224 | tf_op jit(solution)/shard_map/ppermute | solution.py:17
  62.1 273.7 %reduce-scatter.15.cloned.1.call-start = ((), (), s32[]{:S(2)}) async-start(), calls=%async_computation.7 | async-start | bytes 589824
  83.9 26.9 %copy-start.4 = (f32[64]{0:T(128)S(1)}, f32[64]{0:T(128)}, u32[]{:S(2)}) copy-start(f32[64]{0:T(128)} %param.8) | copy-start | bytes 772
  115.9 42.3 %collective-permute-start.4 = (bf16[1,4,1,32,64]{4,3,2,1,0:T(8,128)(2,1)S(1)}, bf16[1,4,1,32,64]{4,3,2,1,0:T(8,128)(2,1)S(1)}, u32[]{:S(2)}, u32[]{:S(2)}) collective-permute-start(bf16[1,4,1,32,64]{4,3,2,1,0:T(8,128)(2,1)S(1)} %get-tuple-element.19), channel_id=1, source_target_pairs={{0,8},{8,16},{16,24},{24,32},{32,40},{40,48},{48,56},{1,9},{9,17},... | collective-permute-start | bytes 49160 | tf_op jit(solution)/shard_map/ppermute | solution.py:16
  119.3 38.8 %collective-permute-start.5 = (bf16[1,4,1,32,64]{4,3,2,1,0:T(8,128)(2,1)S(1)}, bf16[1,4,1,32,64]{4,3,2,1,0:T(8,128)(2,1)S(1)}, u32[]{:S(2)}, u32[]{:S(2)}) collective-permute-start(bf16[1,4,1,32,64]{4,3,2,1,0:T(8,128)(2,1)S(1)} %get-tuple-element.20), channel_id=1, source_target_pairs={{8,0},{16,8},{24,16},{32,24},{40,32},{48,40},{56,48},{9,1},{17,9},... | collective-permute-start | bytes 49160 | tf_op jit(solution)/shard_map/ppermute | solution.py:17
  174.6 301.5 %reduce-scatter.9.cloned.1.call-start = ((), (), s32[]{:S(2)}) async-start(), calls=%async_computation.4 | async-start | bytes 7299072 | tf_op jit(solution)/shard_map/reduce_scatter | solution.py:91
  192.6 18.1 %collective-permute-start.6 = (bf16[1,4,1,32,512]{3,1,2,4,0:T(4,128)(2,1)}, bf16[1,4,1,32,512]{3,1,2,4,0:T(4,128)(2,1)S(1)}, u32[]{:S(2)}, u32[]{:S(2)}) collective-permute-start(bf16[1,4,1,32,512]{3,1,2,4,0:T(4,128)(2,1)} %get-tuple-element.15), channel_id=1, source_target_pairs={{0,8},{8,16},{16,24},{24,32},{32,40},{40,48},{48,56},{1,9},{9,17},... | collective-permute-start | bytes 393224 | tf_op jit(solution)/shard_map/ppermute | solution.py:16
  198.7 22.1 %collective-permute-start.7 = (bf16[1,4,1,32,512]{3,1,2,4,0:T(4,128)(2,1)}, bf16[1,4,1,32,512]{3,1,2,4,0:T(4,128)(2,1)S(1)}, u32[]{:S(2)}, u32[]{:S(2)}) collective-permute-start(bf16[1,4,1,32,512]{3,1,2,4,0:T(4,128)(2,1)} %get-tuple-element.16), channel_id=1, source_target_pairs={{8,0},{16,8},{24,16},{32,24},{40,32},{48,40},{56,48},{9,1},{17,9},... | collective-permute-start | bytes 393224 | tf_op jit(solution)/shard_map/ppermute | solution.py:17
  208.6 527.9 %reduce-scatter.11.cloned.1.call-start = ((), (), s32[]{:S(2)}) async-start(), calls=%async_computation.5 | async-start | bytes 7299072 | tf_op jit(solution)/shard_map/reduce_scatter | solution.py:90
  327.7 408.7 %copy-start.1 = (bf16[27,64,512]{2,1,0:T(8,128)(2,1)S(1)}, bf16[27,64,512]{2,1,0:T(8,128)(2,1)}, u32[]{:S(2)}) copy-start(bf16[27,64,512]{2,1,0:T(8,128)(2,1)} %param.7) | copy-start | bytes 5308420
  335.7 1.3 copy-start.3
Sparse Core Ops, SparseCore 0:
  62.2 47.3 reduce-scatter.12
  174.7 47.0 reduce-scatter.14
  225.0 251.0 reduce-scatter.8
  479.1 257.3 reduce-scatter.10
where the time goes:
time: 758 us; the launch traced here: 743 us
  waiting for transfers between devices  417 us (55%)
  local copies, waits for them, and re-layouts  210 us (28%)
  blocking collectives  35.1 us (5%)
  starting transfers between devices  26.5 us (3%)
  matrix products  25.3 us (3%)
  other arithmetic  14.5 us (2%)
  between operations  14.5 us (2%)
    reduce_scatter x1, waiting for transfers between devices, settle_grads(): lax.psum_scatter(terms[0], ('dp', 'height'), scatter_dimension=1, tiled=T...  260 us
    reduce_scatter x1, waiting for transfers between devices, settle_grads(): lax.psum_scatter(terms[1], ('dp', 'height'), scatter_dimension=1, tiled=T...  138 us
    unnamed x140, local copies, waits for them, and re-layouts  125 us
    another operation x5, local copies, waits for them, and re-layouts, forward_patches(): stacked = jnp.stack(windows, axis=-2)  48.1 us
    all_gather x2, blocking collectives, widen(): return lax.all_gather(value, 'tensor', axis=4, tiled=True)  35.1 us
    dot_general x2, local copies, waits for them, and re-layouts, contract_rows(): lax.dot_general(left, right, (((0,), (0,)), ((), ())), preferred_element_...  20.6 us
    ppermute x4, starting transfers between devices, with_halo(): before = lax.ppermute(last, axis, up)  16.3 us
    dot_general x2, matrix products, contract_rows(): lax.dot_general(left, right, (((0,), (0,)), ((), ())), preferred_element_...  16 us
  transfers between devices with their start and end apart: 12, of which 5 were waited for; matrix products, arithmetic and copies ran while one was open for 30% of the time, Pallas kernels for 0%

commit v1 on v0

v1 whole, which is shorter than its diff:
```python
import math

import jax
import jax.numpy as jnp
from jax import lax
from jax.experimental import pallas as pl
from jax.experimental.pallas import tpu as pltpu
from jax.sharding import PartitionSpec as P

BF = jnp.bfloat16
F32 = jnp.float32
MESH = pl.DeviceIdType.MESH

NX, NZ, NY, NT = 4, 2, 4, 8
TAPS = [(a, b) for a in range(3) for b in range(3)]


def iota(shape, dim):
    return lax.broadcasted_iota(jnp.int32, shape, dim)


def swap(v):
    return pltpu.roll(v, 64, 1)


def low_lane(v):
    return iota(v.shape, 1) < 64


def next_column(v):
    rows = v.shape[0]
    edge = jnp.where(low_lane(v), swap(pltpu.roll(v, 15, 0)), 0.0)
    return jnp.where(iota(v.shape, 0) % 16 == 15, edge, pltpu.roll(v, rows - 1, 0))


def prev_column(v):
    rows = v.shape[0]
    edge = jnp.where(low_lane(v), 0.0, swap(pltpu.roll(v, rows - 15, 0)))
    return jnp.where(iota(v.shape, 0) % 16 == 0, edge, pltpu.roll(v, 1, 0))


def merge(first, second):
    return jnp.where(low_lane(first), first, swap(second))


def merge_high(first, second):
    return jnp.where(low_lane(first), swap(first), second)


def slope(v):
    sig = jax.nn.sigmoid(v)
    return sig * (1.0 + v * (1.0 - sig))


def silu(v):
    return v * jax.nn.sigmoid(v)


def dot(left, right, dims):
    return lax.dot_general(left, right, (dims, ((), ())), preferred_element_type=F32)


def kernel(
    feat, cot, bias, w1_hbm, w2_hbm,
    out_in, out_one, out_two,
    w1, w2, xa, xn, gc, gp, g3c, g3p, part, se, re, sh, rh, acc,
    xs1, xs2, xt1, xt2, sy1, sy2, ry1, ry2, sz1, sz2, rz1, rz2, oz1, oz2,
    featp, cotp,
    w_sem, a_send, a_recv, hu_send, hd_send, hu_recv, hd_recv,
    c_send, c_recv, ce_send, ce_recv, p_send, p_recv, pe_send, pe_recv,
    e_send, e_recv, h_send, h_recv, x1_send, x1_recv, x2_send, x2_recv,
    y1_send, y1_recv, y2_send, y2_recv, z1_send, z1_recv, z2_send, z2_recv,
):
    d = lax.axis_index("dp")
    h = lax.axis_index("height")
    t = lax.axis_index("tensor")
    x = h % NX
    z = h // NX
    mine = x * NT + t

    def remote(src, dst, ssem, rsem, where):
        return pltpu.make_async_remote_copy(
            src_ref=src, dst_ref=dst, send_sem=ssem, recv_sem=rsem,
            device_id=where, device_id_type=MESH,
        )

    copy_w2 = pltpu.make_async_copy(w2_hbm, w2, w_sem.at[0])
    copy_w1 = pltpu.make_async_copy(w1_hbm, w1, w_sem.at[1])
    copy_w2.start()
    copy_w1.start()

    barrier = pltpu.get_barrier_semaphore()

    def greet_slab(k, carry):
        other = (mine + k) % (NX * NT)
        pl.semaphore_signal(
            barrier, inc=1, device_id=(d, z * NX + other // NT, other % NT),
            device_id_type=MESH)
        return carry

    lax.fori_loop(1, NX * NT, greet_slab, 0)
    for k in range(1, NY):
        pl.semaphore_signal(
            barrier, inc=1, device_id=((d + k) % NY, h, t), device_id_type=MESH)
    for k in range(NX):
        pl.semaphore_signal(
            barrier, inc=1, device_id=(d, (1 - z) * NX + k, t), device_id_type=MESH)

    for r in range(2):
        for f in range(4):
            v = feat[0, f, r].astype(F32)
            v = jnp.concatenate([v[:16], v[16:]], axis=-1)
            featp[r, f] = v
            xa[t, 1 + r, f] = silu(v).astype(BF)
            c = cot[0, f, r].astype(F32)
            c = jnp.concatenate([c[:16], c[16:]], axis=-1)
            cotp[r, f] = c
            gc[2 * x + 1 + r, f] = c.astype(BF)

    zero_row = jnp.zeros((4, 16, 128), BF)
    for ref in (gc, gp):
        @pl.when(z == 0)
        def _():
            ref[0] = zero_row

        @pl.when(z == 1)
        def _():
            ref[9] = zero_row

    @pl.when(h == 0)
    def _():
        for k in range(NT):
            xa[k, 0] = zero_row

    @pl.when(h == NX * NZ - 1)
    def _():
        for k in range(NT):
            xa[k, 3] = zero_row

    pl.semaphore_wait(barrier, NX * NT - 1 + NY - 1 + NX)

    def gather_act(k):
        return remote(xa.at[t, pl.ds(1, 2)], xa.at[t, pl.ds(1, 2)],
                      a_send.at[k - 1], a_recv.at[t], (d, h, (t + k) % NT))

    def gather_rows(ref, ssem, rsem, k):
        rows = ref.at[pl.ds(2 * x + 1, 2)]
        return remote(rows, rows, ssem.at[k - 1], rsem.at[x],
                      (d, z * NX + (x + k) % NX, t))

    def edge_up(ref, ssem, rsem, k):
        return remote(ref.at[8], ref.at[0], ssem.at[k], rsem.at[0], (d, NX + k, t))

    def edge_down(ref, ssem, rsem, k):
        return remote(ref.at[1], ref.at[9], ssem.at[k], rsem.at[0], (d, k, t))

    def on_edges(ref, ssem, rsem, act):
        @pl.when(h == NX - 1)
        def _():
            for k in range(NX):
                act(edge_up(ref, ssem, rsem, k))

        @pl.when(h == NX)
        def _():
            for k in range(NX):
                act(edge_down(ref, ssem, rsem, k))

    def start(copy):
        copy.start()

    def wait_send(copy):
        copy.wait_send()

    def send_rows(ref, ssem, rsem, esend, erecv):
        for k in (1, 3, 2):
            gather_rows(ref, ssem, rsem, k).start()
        on_edges(ref, esend, erecv, start)

    def await_rows(ref, ssem, rsem, esend, erecv):
        for k in range(1, NX):
            other = (x + k) % NX
            rows = ref.at[pl.ds(2 * other + 1, 2)]
            remote(rows, rows, ssem.at[0], rsem.at[other], (d, h, t)).wait_recv()
        edge = ref.at[0]
        remote(edge, edge, esend.at[0], erecv.at[0], (d, h, t)).wait_recv()

    def finish_rows(ref, ssem, rsem, esend, erecv):
        for k in range(1, NX):
            gather_rows(ref, ssem, rsem, k).wait_send()
        on_edges(ref, esend, erecv, wait_send)

    def scatter(src, dst, ssem, rsem, k):
        other = (t + k) % NT
        return remote(src.at[other], dst.at[t], ssem.at[k - 1], rsem.at[t],
                      (d, h, other))

    def await_block(dst, ssem, rsem, k):
        other = (t + k) % NT
        remote(dst.at[other], dst.at[other], ssem.at[0], rsem.at[other],
               (d, h, t)).wait_recv()

    def send_act(src, dst, ssem, rsem, k):
        other = (mine + k) % (NX * NT)
        return remote(src.at[other // NT], dst.at[x, t], ssem.at[k - 1],
                      rsem.at[mine], (d, z * NX + other // NT, other % NT))

    def send_acts(src, dst, ssem, rsem):
        def step(k, carry):
            send_act(src, dst, ssem, rsem, k).start()
            return carry
        lax.fori_loop(1, NX * NT, step, 0)

    def await_acts(dst, ssem, rsem):
        def step(k, carry):
            other = (mine + k) % (NX * NT)
            block = dst.at[other // NT, other % NT]
            remote(block, block, ssem.at[0], rsem.at[other], (d, h, t)).wait_recv()
            return carry
        lax.fori_loop(1, NX * NT, step, 0)

    def finish_acts(src, dst, ssem, rsem):
        def step(k, carry):
            send_act(src, dst, ssem, rsem, k).wait_send()
            return carry
        lax.fori_loop(1, NX * NT, step, 0)

    def spread(rows, dst):
        v = rows[...].astype(F32).reshape(640, 128)
        up, down = next_column(v), prev_column(v)
        nothing = jnp.zeros_like(v)
        pieces = (
            (merge(up, v), merge(down, nothing)),
            (merge_high(up, v), merge_high(down, nothing)),
        )
        for half in range(2):
            for side in range(2):
                dst[half, :, 0:4, :, 128 * side:128 * side + 128] = (
                    pieces[half][side].astype(BF).reshape(10, 4, 16, 128))
            dst[half, :, 4:6] = jnp.zeros((10, 2, 16, 256), BF)

    def transposed_conv(g3, w, dst):
        for a, b in sorted(TAPS, reverse=True):
            n = 2 + a
            left = g3[:, pl.ds(2 * x + 2 - b, 2), 2 - a:4, :, 0:192]
            tap = 3 * (3 * a + b)
            right = w[tap:tap + 3].reshape(192, 512)
            v = dot(left.reshape(64 * n, 192), right, ((1,), (0,)))
            v = v.reshape(2, 2, n, 16, 512)
            if (a, b) == (2, 2):
                part[...] = v
            else:
                part[:, :, 0:n] = part[:, :, 0:n] + v

    def split_part(dst):
        for p in range(4):
            low = part[0, :, :, :, 128 * p:128 * p + 128].reshape(128, 128)
            high = part[1, :, :, :, 128 * p:128 * p + 128].reshape(128, 128)
            dst[2 * p] = merge(low, high).astype(BF).reshape(2, 4, 16, 128)
            dst[2 * p + 1] = merge_high(low, high).astype(BF).reshape(2, 4, 16, 128)

    def transposed(packed, src, dst):
        v = jnp.transpose(packed)
        v = jnp.concatenate([v[:64], v[64:]], axis=1).astype(BF)
        src[...] = v.reshape(4, 16, 256)
        dst[x, t] = src[x]

    def kernel_grad(xt, g3, sy):
        for a, b in TAPS:
            total = None
            for s in range(NX):
                left = xt[s].reshape(128, 256)
                right = g3[:, 2 * s + 2 - b:2 * s + 4 - b, 2 - a:6 - a, :, 0:192]
                v = dot(left, right.reshape(256, 192), ((1,), (0,)))
                total = v if total is None else total + v
            sy[:, 3 * a + b] = total.astype(BF).reshape(8, 16, 192)

    def send_y(sy, ry, ssem, rsem, k):
        other = (d + k) % NY
        return remote(sy.at[pl.ds(2 * other, 2)], ry.at[d], ssem.at[k - 1],
                      rsem.at[d], (other, h, t))

    def await_y(ry, ssem, rsem):
        for k in range(1, NY):
            other = (d + k) % NY
            remote(ry.at[other], ry.at[other], ssem.at[0], rsem.at[other],
                   (d, h, t)).wait_recv()

    def send_z(sz, rz, ssem, rsem):
        return remote(sz, rz, ssem.at[0], rsem.at[0], (d, (1 - z) * NX + x, t))

    def sum_y(sy, ry, which):
        total = sy[2 * d + which].astype(F32)
        for k in range(1, NY):
            total = total + ry[(d + k) % NY, which].astype(F32)
        return total

    scale = 1.0 / math.sqrt(4 * 4 * 16 * 32)

    def write_grad(oz, rz, out):
        v = (oz[...] + rz[...].astype(F32)) * scale
        for k in range(9):
            for e in range(3):
                out[3 * k + e] = v[k, :, 64 * e:64 * e + 64]

    send_rows(gc, c_send, c_recv, ce_send, ce_recv)
    for k in (1, 7, 2, 6, 3, 5, 4):
        gather_act(k).start()

    await_rows(gc, c_send, c_recv, ce_send, ce_recv)
    spread(gc, g3c)
    copy_w2.wait()
    transposed_conv(g3c, w2, part)
    split_part(se)
    for k in range(1, NT):
        scatter(se, re, e_send, e_recv, k).start()

    def halo_up(k):
        return remote(xa.at[k, 1], xa.at[k, 3], hu_send.at[k], hu_recv.at[k],
                      (d, h - 1, t))

    def halo_down(k):
        return remote(xa.at[k, 2], xa.at[k, 0], hd_send.at[k], hd_recv.at[k],
                      (d, h + 1, t))

    for k in (0, 1, 7, 2, 6, 3, 5, 4):
        other = (t + k) % NT
        if k:
            rows = xa.at[other, pl.ds(1, 2)]
            remote(rows, rows, a_send.at[0], a_recv.at[other], (d, h, t)).wait_recv()

        @pl.when(h > 0)
        def _():
            halo_up(other).start()

        @pl.when(h < NX * NZ - 1)
        def _():
            halo_down(other).start()

    transposed(xa[t, 1:3].astype(F32).reshape(128, 128), xs1, xt1)
    send_acts(xs1, xt1, x1_send, x1_recv)

    @pl.when(h < NX * NZ - 1)
    def _():
        for k in range(NT):
            remote(xa.at[k, 3], xa.at[k, 3], hu_send.at[0], hu_recv.at[k],
                   (d, h, t)).wait_recv()

    @pl.when(h > 0)
    def _():
        for k in range(NT):
            remote(xa.at[k, 0], xa.at[k, 0], hd_send.at[0], hd_recv.at[k],
                   (d, h, t)).wait_recv()

    for p in range(4):
        first = xa[2 * p].astype(F32).reshape(256, 128)
        second = xa[2 * p + 1].astype(F32).reshape(256, 128)
        xn[0, :, :, :, 128 * p:128 * p + 128] = (
            merge(first, second).astype(BF).reshape(4, 4, 16, 128))
        xn[1, :, :, :, 128 * p:128 * p + 128] = (
            merge_high(first, second).astype(BF).reshape(4, 4, 16, 128))

    copy_w1.wait()
    acc[...] = jnp.zeros_like(acc)
    for a, b in TAPS:
        n = 2 + a
        left = xn[:, b:b + 2, 0:n].reshape(64 * n, 512)
        tap = 3 * (3 * a + b)
        right = w1[tap:tap + 3].reshape(192, 512)
        v = dot(left, right, ((1,), (1,))).reshape(2, 2, n, 16, 192)
        acc[:, :, 2 - a:4, :, 0:192] = acc[:, :, 2 - a:4, :, 0:192] + v
    low0 = acc[0, :, :, :, 0:128].reshape(128, 128)
    low1 = acc[0, :, :, :, 128:256].reshape(128, 128)
    high0 = acc[1, :, :, :, 0:128].reshape(128, 128)
    high1 = acc[1, :, :, :, 128:256].reshape(128, 128)
    wide_bias = jnp.concatenate([bias[...], bias[...]], axis=1)
    preact = (prev_column(merge(low0, high0)) + merge_high(low0, high0)
              + next_column(merge(low1, high1)) + wide_bias)
    act_two = silu(preact).astype(BF).astype(F32)

    for k in range(1, NT):
        await_block(re, e_send, e_recv, k)
    back = se[t].astype(F32)
    for k in range(1, NT):
        back = back + re[(t + k) % NT].astype(F32)
    grad_pre = back.reshape(128, 128) * slope(preact)
    gp[pl.ds(2 * x + 1, 2)] = grad_pre.astype(BF).reshape(2, 4, 16, 128)
    send_rows(gp, p_send, p_recv, pe_send, pe_recv)
    transposed(act_two, xs2, xt2)
    send_acts(xs2, xt2, x2_send, x2_recv)

    await_rows(gp, p_send, p_recv, pe_send, pe_recv)
    spread(gp, g3p)
    transposed_conv(g3p, w1, part)
    split_part(sh)
    for k in range(1, NT):
        scatter(sh, rh, h_send, h_recv, k).start()

    await_acts(xt1, x1_send, x1_recv)
    kernel_grad(xt1, g3p, sy1)
    for k in (1, 3, 2):
        send_y(sy1, ry1, y1_send, y1_recv, k).start()
    await_acts(xt2, x2_send, x2_recv)
    kernel_grad(xt2, g3c, sy2)
    for k in (1, 3, 2):
        send_y(sy2, ry2, y2_send, y2_recv, k).start()

    await_y(ry1, y1_send, y1_recv)
    sz1[...] = sum_y(sy1, ry1, 1 - z).astype(BF)
    send_z(sz1, rz1, z1_send, z1_recv).start()
    oz1[...] = sum_y(sy1, ry1, z)

    for k in range(1, NT):
        await_block(rh, h_send, h_recv, k)
    back = sh[t].astype(F32)
    for k in range(1, NT):
        back = back + rh[(t + k) % NT].astype(F32)
    grad_in = cotp[...] + back * slope(featp[...])
    for r in range(2):
        for f in range(4):
            out_in[0, f, r, 0:16] = grad_in[r, f, :, 0:64].astype(BF)
            out_in[0, f, r, 16:32] = grad_in[r, f, :, 64:128].astype(BF)

    await_y(ry2, y2_send, y2_recv)
    sz2[...] = sum_y(sy2, ry2, 1 - z).astype(BF)
    send_z(sz2, rz2, z2_send, z2_recv).start()
    oz2[...] = sum_y(sy2, ry2, z)

    send_z(sz1, rz1, z1_send, z1_recv).wait_recv()
    write_grad(oz1, rz1, out_one)
    send_z(sz2, rz2, z2_send, z2_recv).wait_recv()
    write_grad(oz2, rz2, out_two)

    for k in range(1, NT):
        gather_act(k).wait_send()
        scatter(se, re, e_send, e_recv, k).wait_send()
        scatter(sh, rh, h_send, h_recv, k).wait_send()

    @pl.when(h > 0)
    def _():
        for k in range(NT):
            halo_up(k).wait_send()

    @pl.when(h < NX * NZ - 1)
    def _():
        for k in range(NT):
            halo_down(k).wait_send()

    finish_rows(gc, c_send, c_recv, ce_send, ce_recv)
    finish_rows(gp, p_send, p_recv, pe_send, pe_recv)
    finish_acts(xs1, xt1, x1_send, x1_recv)
    finish_acts(xs2, xt2, x2_send, x2_recv)
    for k in range(1, NY):
        send_y(sy1, ry1, y1_send, y1_recv, k).wait_send()
        send_y(sy2, ry2, y2_send, y2_recv, k).wait_send()
    send_z(sz1, rz1, z1_send, z1_recv).wait_send()
    send_z(sz2, rz2, z2_send, z2_recv).wait_send()


def local(features, cotangent, conv_one, bias_one, conv_two):
    vmem = pl.BlockSpec(memory_space=pltpu.VMEM)
    hbm = pl.BlockSpec(memory_space=pl.ANY)
    dma = pltpu.SemaphoreType.DMA
    block = (2, 4, 16, 128)
    scratch = [
        pltpu.VMEM((27, 64, 512), BF), pltpu.VMEM((27, 64, 512), BF),
        pltpu.VMEM((8, 4, 4, 16, 128), BF), pltpu.VMEM((2, 4, 4, 16, 512), BF),
        pltpu.VMEM((10, 4, 16, 128), BF), pltpu.VMEM((10, 4, 16, 128), BF),
        pltpu.VMEM((2, 10, 6, 16, 256), BF), pltpu.VMEM((2, 10, 6, 16, 256), BF),
        pltpu.VMEM((2, 2, 4, 16, 512), F32),
        pltpu.VMEM((8,) + block, BF), pltpu.VMEM((8,) + block, BF),
        pltpu.VMEM((8,) + block, BF), pltpu.VMEM((8,) + block, BF),
        pltpu.VMEM((2, 2, 4, 16, 256), F32),
        pltpu.VMEM((4, 16, 256), BF), pltpu.VMEM((4, 16, 256), BF),
        pltpu.VMEM((4, 8, 16, 256), BF), pltpu.VMEM((4, 8, 16, 256), BF),
        pltpu.VMEM((8, 9, 16, 192), BF), pltpu.VMEM((8, 9, 16, 192), BF),
        pltpu.VMEM((4, 2, 9, 16, 192), BF), pltpu.VMEM((4, 2, 9, 16, 192), BF),
        pltpu.VMEM((9, 16, 192), BF), pltpu.VMEM((9, 16, 192), BF),
        pltpu.VMEM((9, 16, 192), BF), pltpu.VMEM((9, 16, 192), BF),
        pltpu.VMEM((9, 16, 192), F32), pltpu.VMEM((9, 16, 192), F32),
        pltpu.VMEM(block, F32), pltpu.VMEM(block, F32),
        dma((2,)), dma((7,)), dma((8,)),
        dma((8,)), dma((8,)), dma((8,)), dma((8,)),
        dma((3,)), dma((4,)), dma((4,)), dma((1,)),
        dma((3,)), dma((4,)), dma((4,)), dma((1,)),
        dma((7,)), dma((8,)), dma((7,)), dma((8,)),
        dma((31,)), dma((32,)), dma((31,)), dma((32,)),
        dma((3,)), dma((4,)), dma((3,)), dma((4,)),
        dma((1,)), dma((1,)), dma((1,)), dma((1,)),
    ]
    return pl.pallas_call(
        kernel,
        out_shape=(
            jax.ShapeDtypeStruct((1, 4, 2, 32, 64), BF),
            jax.ShapeDtypeStruct((27, 16, 64), F32),
            jax.ShapeDtypeStruct((27, 16, 64), F32),
        ),
        in_specs=[vmem, vmem, vmem, hbm, hbm],
        out_specs=(vmem, vmem, vmem),
        scratch_shapes=scratch,
        compiler_params=pltpu.CompilerParams(
            collective_id=0, has_side_effects=True, vmem_limit_bytes=40 * 1024 * 1024
        ),
    )(features, cotangent, bias_one.reshape(1, -1), conv_one, conv_two)


def solution(mesh):
    in_specs = (
        P("dp", None, "height", None, "tensor"),
        P("dp", None, "height", None, "tensor"),
        P(None, "tensor", None),
        P("tensor"),
        P(None, "tensor", None),
    )
    out_specs = (
        P("dp", None, "height", None, "tensor"),
        P(None, ("dp", "height"), "tensor"),
        P(None, ("dp", "height"), "tensor"),
    )
    return jax.shard_map(local, mesh=mesh, in_specs=in_specs, out_specs=out_specs, check_vma=False)
```

time: 758 us -> 73.4 us (0.10)
  the two profiles are of different devices: /device:TPU:2 before, /device:TPU:1 now
where the time goes in v1:
time: 73.4 us; the launch traced here: 73.1 us
  Pallas kernels  65.2 us (89%)
  local copies, waits for them, and re-layouts  7.28 us (10%)
    pallas_call x1, Pallas kernels, local(): pl.pallas_call(kernel, out_shape=(jax.ShapeDtypeStruct((1, 4, 2, 32, 64),...  65.2 us
    unnamed x13, local copies, waits for them, and re-layouts  7.28 us

profile of v1, /device:TPU:1, one launch (start us, length us, event | category | flops | bytes accessed | tf_op | source)
XLA Modules:
  0.0 73.1 jit_solution(7139373865581578394)
XLA Ops:
  0.6 0.0 copy-start
  0.6 1.5 %copy-done = bf16[27,64,512]{2,1,0:T(8,128)(2,1)S(1)} copy-done((bf16[27,64,512]{2,1,0:T(8,128)(2,1)S(1)}, bf16[27,64,512]{2,1,0:T(8,128)(2,1)}, u32[]{:S(2)}) %copy-start) | copy-done | bytes 1769496
  2.1 0.0 copy-start.1
  2.1 1.5 %copy-done.1 = bf16[27,64,512]{2,1,0:T(8,128)(2,1)S(1)} copy-done((bf16[27,64,512]{2,1,0:T(8,128)(2,1)S(1)}, bf16[27,64,512]{2,1,0:T(8,128)(2,1)}, u32[]{:S(2)}) %copy-start.1) | copy-done | bytes 1769496
  3.6 0.0 copy-start.2
  3.6 0.8 %copy-done.2 = bf16[1,4,2,32,64]{4,3,2,1,0:T(8,128)(2,1)S(1)} copy-done((bf16[1,4,2,32,64]{4,3,2,1,0:T(8,128)(2,1)S(1)}, bf16[1,4,2,32,64]{4,3,2,1,0:T(8,128)(2,1)}, u32[]{:S(2)}) %copy-start.2) | copy-done | bytes 32792
  4.4 0.0 copy-start.3
  4.4 0.8 %copy-done.3 = bf16[1,4,2,32,64]{4,3,2,1,0:T(8,128)(2,1)S(1)} copy-done((bf16[1,4,2,32,64]{4,3,2,1,0:T(8,128)(2,1)S(1)}, bf16[1,4,2,32,64]{4,3,2,1,0:T(8,128)(2,1)}, u32[]{:S(2)}) %copy-start.3) | copy-done | bytes 32792
  5.3 0.0 copy-start.4
  5.3 0.7 copy-done.4
  5.9 65.2 %shard_map.76 = (bf16[1,4,2,32,64]{4,3,2,1,0:T(8,128)(2,1)S(1)}, f32[27,16,64]{2,1,0:T(8,128)S(1)}, f32[27,16,64]{2,1,0:T(8,128)S(1)}) custom-call(bf16[1,4,2,32,64]{4,3,2,1,0:T(8,128)(2,1)S(1)} %copy-done.2, bf16[1,4,2,32,64]{4,3,2,1,0:T(8,128)(2,1)S(1)} %copy-done.3, f32[1,64]{1,0:T(1,128)S(1)} %bitcast.1, bf16[27,64,512]{2,1,0:T(8,128)(2,1)S(1)} %copy-done, ...), custom_call_target="tpu_custom_call" | custom-call | tf_op jit(solution)/shard_map/pallas_call | solution.py:490
  71.1 0.6 copy.11
  71.8 0.7 copy.12
  72.4 0.7 copy.13
Async XLA Ops:
  0.6 1.5 %copy-start = (bf16[27,64,512]{2,1,0:T(8,128)(2,1)S(1)}, bf16[27,64,512]{2,1,0:T(8,128)(2,1)}, u32[]{:S(2)}) copy-start(bf16[27,64,512]{2,1,0:T(8,128)(2,1)} %w1_hbm.1) | copy-start | bytes 5308420
  2.1 1.5 %copy-start.1 = (bf16[27,64,512]{2,1,0:T(8,128)(2,1)S(1)}, bf16[27,64,512]{2,1,0:T(8,128)(2,1)}, u32[]{:S(2)}) copy-start(bf16[27,64,512]{2,1,0:T(8,128)(2,1)} %w2_hbm.1) | copy-start | bytes 5308420
  3.6 0.8 %copy-start.2 = (bf16[1,4,2,32,64]{4,3,2,1,0:T(8,128)(2,1)S(1)}, bf16[1,4,2,32,64]{4,3,2,1,0:T(8,128)(2,1)}, u32[]{:S(2)}) copy-start(bf16[1,4,2,32,64]{4,3,2,1,0:T(8,128)(2,1)} %feat.1) | copy-start | bytes 98308
  4.4 0.8 %copy-start.3 = (bf16[1,4,2,32,64]{4,3,2,1,0:T(8,128)(2,1)S(1)}, bf16[1,4,2,32,64]{4,3,2,1,0:T(8,128)(2,1)}, u32[]{:S(2)}) copy-start(bf16[1,4,2,32,64]{4,3,2,1,0:T(8,128)(2,1)} %cot.1) | copy-start | bytes 98308
  5.3 0.7 copy-start.4

commit v2 on v0

v2 whole, which is shorter than its diff:
```python
import math

import jax
import jax.numpy as jnp
from jax import lax
from jax.experimental import pallas as pl
from jax.experimental.pallas import tpu as pltpu
from jax.sharding import PartitionSpec as P

BF = jnp.bfloat16
F32 = jnp.float32
MESH = pl.DeviceIdType.MESH

NX, NZ, NY, NT = 4, 2, 4, 8
SENDS, RECVS = 136, 160
TAPS = [(a, b) for a in range(3) for b in range(3)]


def iota(shape, dim):
    return lax.broadcasted_iota(jnp.int32, shape, dim)


def swap(v):
    return pltpu.roll(v, 64, 1)


def low_lane(v):
    return iota(v.shape, 1) < 64


def next_column(v):
    rows = v.shape[0]
    edge = jnp.where(low_lane(v), swap(pltpu.roll(v, 15, 0)), 0.0)
    return jnp.where(iota(v.shape, 0) % 16 == 15, edge, pltpu.roll(v, rows - 1, 0))


def prev_column(v):
    rows = v.shape[0]
    edge = jnp.where(low_lane(v), 0.0, swap(pltpu.roll(v, rows - 15, 0)))
    return jnp.where(iota(v.shape, 0) % 16 == 0, edge, pltpu.roll(v, 1, 0))


def merge(first, second):
    return jnp.where(low_lane(first), first, swap(second))


def merge_high(first, second):
    return jnp.where(low_lane(first), swap(first), second)


def slope(v):
    sig = jax.nn.sigmoid(v)
    return sig * (1.0 + v * (1.0 - sig))


def silu(v):
    return v * jax.nn.sigmoid(v)


def dot(left, right, dims):
    return lax.dot_general(left, right, (dims, ((), ())), preferred_element_type=F32)


def kernel(
    feat_hbm, cot_hbm, bias_hbm, w1_hbm, w2_hbm,
    in_hbm, one_hbm, two_hbm,
    feat, cot, bias, w1, w2, xa, xn, cn, gn, gc, gp, g3n, g3c, g3p, part, acc,
    own, e1, e1r, e2, e2r, h1, h1r, h2, h2r,
    xs1, xs2, xr2, xt1, xt2, sf1, sf2, sy1, sy2, ry1, ry2,
    featp, cotp, out_in, out_one, out_two, in_sem, out_sem, send_sem, recv_sem,
):
    d = lax.axis_index("dp")
    h = lax.axis_index("height")
    t = lax.axis_index("tensor")
    x = h % NX
    z = h // NX
    k = t // 2
    c = t % 2
    home = c == z
    partner = (1 - z) * NX + x
    here = (d, h, t)
    sibling = (d, h, 2 * k + 1 - c)

    copies = [
        pltpu.make_async_copy(src, dst, in_sem.at[i]) for i, (src, dst) in enumerate(
            [(feat_hbm, feat), (cot_hbm, cot), (bias_hbm, bias), (w2_hbm, w2), (w1_hbm, w1)])
    ]
    for copy in copies:
        copy.start()

    counts = {"send": 0, "recv": 0}

    def reserve(kind, n):
        base = counts[kind]
        counts[kind] = base + n
        return base

    def remote(src, dst, s, r, where):
        return pltpu.make_async_remote_copy(
            src_ref=src, dst_ref=dst, send_sem=send_sem.at[s], recv_sem=recv_sem.at[r],
            device_id=where, device_id_type=MESH,
        )

    unfinished = []

    def post(src, dst, r, where, when=None):
        s = reserve("send", 1)

        def make():
            return remote(src, dst, s, r, where)

        def begin():
            make().start()

        def finish():
            make().wait_send()

        if when is None:
            begin()
        else:
            pl.when(when)(begin)
        unfinished.append((finish, when))

    def await_into(dst, r):
        remote(dst, dst, 0, r, here).wait_recv()

    barrier = pltpu.get_barrier_semaphore()

    def greet(where):
        pl.semaphore_signal(barrier, inc=1, device_id=where, device_id_type=MESH)

    for i in range(NX):
        for j in range(4):
            if i or j:
                greet((d, z * NX + (x + i) % NX, 2 * ((k + j) % 4) + c))
        greet((d, (1 - z) * NX + i, t))
    for i in range(1, NY):
        greet(((d + i) % NY, h, t))
    greet(sibling)

    copies[0].wait()
    copies[1].wait()
    copies[2].wait()
    for r in range(2):
        for f in range(4):
            v = feat[0, f, r].astype(F32)
            v = jnp.concatenate([v[:16], v[16:]], axis=-1)
            featp[r, f] = v
            xa[c, k, 1 + r, f] = silu(v).astype(BF)
            v = cot[0, f, r].astype(F32)
            v = jnp.concatenate([v[:16], v[16:]], axis=-1)
            cotp[r, f] = v
            cn[1 + r, f] = v.astype(BF)
            gc[2 * h + r, f] = v.astype(BF)

    zero_row = jnp.zeros((4, 16, 128), BF)
    @pl.when(h == 0)
    def _():
        for i in range(2):
            for j in range(4):
                xa[i, j, 0] = zero_row
        cn[0] = zero_row
        gn[0] = zero_row

    @pl.when(h == NX * NZ - 1)
    def _():
        for i in range(2):
            for j in range(4):
                xa[i, j, 3] = zero_row
        cn[3] = zero_row
        gn[3] = zero_row

    for ref in (g3c, g3p):
        for i in range(2):
            for j in (0, 17):
                ref[i, j] = jnp.zeros((6, 16, 256), BF)
            for j in (4, 5):
                ref[i, :, j] = jnp.zeros((18, 16, 256), BF)
    acc[...] = jnp.zeros_like(acc)

    pl.semaphore_wait(barrier, NX * 4 - 1 + NX + NY - 1 + 1)

    def spread(rows, dst, first):
        n = rows.shape[0]
        v = rows[...].astype(F32).reshape(64 * n, 128)
        up, down = next_column(v), prev_column(v)
        nothing = jnp.zeros_like(v)
        pieces = (
            (merge(up, v), merge(down, nothing)),
            (merge_high(up, v), merge_high(down, nothing)),
        )
        for half in range(2):
            for side in range(2):
                dst[half, first:first + n, 0:4, :, 128 * side:128 * side + 128] = (
                    pieces[half][side].astype(BF).reshape(n, 4, 16, 128))

    def transposed_conv(w):
        for a, b in sorted(TAPS, reverse=True):
            n = 2 + a
            left = g3n[:, 2 - b:4 - b, 2 - a:4, :, 0:192]
            tap = 3 * (3 * a + b)
            right = w[tap:tap + 3].reshape(192, 512)
            v = dot(left.reshape(64 * n, 192), right, ((1,), (0,)))
            v = v.reshape(2, 2, n, 16, 512)
            if (a, b) == (2, 2):
                part[...] = v
            else:
                part[:, :, 0:n] = part[:, :, 0:n] + v

    def scatter_begin(first, first_in):
        base = reserve("recv", 4)
        for i in range(4):
            low = part[0, :, :, :, 128 * i:128 * i + 128].reshape(128, 128)
            high = part[1, :, :, :, 128 * i:128 * i + 128].reshape(128, 128)
            even, odd = merge(low, high), merge_high(low, high)
            keep = jnp.where(c == 0, even, odd)
            give = jnp.where(c == 0, odd, even)
            own[i] = keep.reshape(2, 4, 16, 128)
            first[i] = give.astype(BF).reshape(2, 4, 16, 128)
            post(first.at[i], first_in.at[i], base + i, sibling)
        return base

    def scatter_on(base, first_in, second, second_in):
        after = reserve("recv", 4)
        for j in (2, 1, 3, 0):
            chip = (k + j) % 4
            await_into(first_in.at[chip], base + chip)
            v = own[chip] + first_in[chip].astype(F32)
            if j:
                second[chip] = v.astype(BF)
                post(second.at[chip], second_in.at[k], after + k, (d, h, 2 * chip + c))
            else:
                own[chip] = v
        return after

    def scatter_end(base, second_in):
        total = own[k]
        for j in range(1, 4):
            chip = (k + j) % 4
            await_into(second_in.at[chip], base + chip)
            total = total + second_in[chip].astype(F32)
        return total

    def near_begin(ref):
        base = reserve("recv", 2)
        post(ref.at[1], ref.at[3], base, (d, h - 1, t), h > 0)
        post(ref.at[2], ref.at[0], base + 1, (d, h + 1, t), h < NX * NZ - 1)
        return base

    def near_end(ref, base):
        @pl.when(h < NX * NZ - 1)
        def _():
            await_into(ref.at[3], base)

        @pl.when(h > 0)
        def _():
            await_into(ref.at[0], base + 1)

    def rows_of(ref, source):
        return ref.at[pl.ds(2 * source, 2)]

    def far_begin(ref):
        base = reserve("recv", 8)
        rows = rows_of(ref, h)
        post(rows, rows, base + h, (d, partner, t))
        for j in (1, 3, 2):
            post(rows, rows, base + h, (d, z * NX + (x + j) % NX, t))
        return base

    def far_relay(ref, base):
        rows = rows_of(ref, partner)
        await_into(rows, base + partner)
        for j in (1, 3, 2):
            post(rows, rows, base + partner, (d, z * NX + (x + j) % NX, t))

    def far_end(ref, base):
        for i in (z, 1 - z):
            for j in range(1, NX):
                other = i * NX + (x + j) % NX
                await_into(rows_of(ref, other), base + other)

    def transposed(packed):
        v = jnp.transpose(packed)
        return jnp.concatenate([v[:64], v[64:]], axis=1).astype(BF).reshape(4, 16, 256)

    def grad_begin(xt, g3, sf, sy, ry):
        base = reserve("recv", 12)
        for a in range(3):
            sides = []
            for b in range(3):
                total = None
                for s in range(NX * NZ):
                    left = xt[s // NX, s % NX].reshape(64, 256)
                    right = g3[:, 2 * s + 2 - b:2 * s + 4 - b, 2 - a:6 - a]
                    v = dot(left, right.reshape(256, 256), ((1,), (0,)))
                    total = v if total is None else total + v
                tile = total[:, 0:128].reshape(4, 16, 128)
                sf[:, a, b] = tile
                sy[:, a, b] = tile.astype(BF)
                sides.append(total[:, 128:256])
            for i, v in ((3, merge(sides[0], sides[1])), (4, sides[2])):
                tile = v.reshape(4, 16, 128)
                sf[:, a, i] = tile
                sy[:, a, i] = tile.astype(BF)
            for j in (2, 1, 3):
                other = (d + j) % NY
                post(sy.at[other, a], ry.at[d, a], base + 4 * a + d, (other, h, t))
        return base

    scale = 1.0 / math.sqrt(4 * 4 * 16 * 32)

    def grad_end(base, sf, ry, out):
        for a in range(3):
            v = sf[d, a]
            for j in range(1, NY):
                other = (d + j) % NY
                await_into(ry.at[other, a], base + 4 * a + other)
                v = v + ry[other, a].astype(F32)
            v = v * scale
            for b in range(3):
                tap = 9 * a + 3 * b
                out[tap] = v[b, :, 0:64]
                out[tap + 1] = v[b, :, 64:128]
                side = v[3 + b // 2]
                out[tap + 2] = side[:, 64:128] if b == 1 else side[:, 0:64]

    a_base = reserve("recv", 8)
    up_base = reserve("recv", 8)
    down_base = reserve("recv", 8)

    not_first, not_last = h > 0, h < NX * NZ - 1

    def halo(chip, up_when, down_when):
        post(xa.at[c, chip, 1], xa.at[c, chip, 3], up_base + 4 * c + chip,
             (d, h - 1, t), up_when)
        post(xa.at[c, chip, 2], xa.at[c, chip, 0], down_base + 4 * c + chip,
             (d, h + 1, t), down_when)

    mine = xa.at[c, k, pl.ds(1, 2)]
    for j in (2, 1, 3):
        post(mine, mine, a_base + 4 * c + k, (d, h, 2 * ((k + j) % 4) + c))
    post(mine, mine, a_base + 4 * c + k, sibling)
    cn_base = near_begin(cn)
    halo(k, not_first, not_last)

    near_end(cn, cn_base)
    spread(cn, g3n, 0)

    for j in (1, 3, 2):
        chip = (k + j) % 4
        rows = xa.at[c, chip, pl.ds(1, 2)]
        await_into(rows, a_base + 4 * c + chip)
        post(rows, rows, a_base + 4 * c + chip, sibling)
        halo(chip, not_first & (h != NX), not_last & (h != NX - 1))

    @pl.when(h == NX)
    def _():
        await_into(xa.at[c, k, 0], down_base + 4 * c + k)

    @pl.when(h == NX - 1)
    def _():
        await_into(xa.at[c, k, 3], up_base + 4 * c + k)

    for j in (2, 1, 3):
        peer = (d, h, 2 * ((k + j) % 4) + c)
        post(xa.at[c, k, 0], xa.at[c, k, 0], down_base + 4 * c + k, peer, h == NX)
        post(xa.at[c, k, 3], xa.at[c, k, 3], up_base + 4 * c + k, peer, h == NX - 1)

    for i in range(4):
        xs1[:, i] = transposed(xa[c, i, 1:3].astype(F32).reshape(128, 128))
    x1_base = reserve("recv", 8)
    for j in (2, 1, 3, 0):
        other = (x + j) % NX
        post(xs1.at[other], xt1.at[z, x], x1_base + h, (d, c * NX + other, t),
             None if j else jnp.logical_not(home))

    @pl.when(home)
    def _():
        xt1[z, x] = xs1[x]

    copies[3].wait()
    transposed_conv(w2)
    e_base = scatter_begin(e1, e1r)
    c_base = far_begin(gc)

    for row, base, when, edge in (
        (3, up_base, not_last, NX - 1), (0, down_base, not_first, NX)
    ):
        for j in range(4):
            chip = (k + j) % 4

            @pl.when(when if j else when & (h != edge))
            def _():
                await_into(xa.at[c, chip, row], base + 4 * c + chip)

    up_sib = reserve("recv", 1)
    post(xa.at[c, :, 3], xa.at[c, :, 3], up_sib, sibling, not_last)
    down_sib = reserve("recv", 1)
    post(xa.at[c, :, 0], xa.at[c, :, 0], down_sib, sibling, not_first)

    e_base = scatter_on(e_base, e1r, e2, e2r)

    for j in range(4):
        chip = (k + j) % 4
        await_into(xa.at[1 - c, chip, pl.ds(1, 2)], a_base + 4 * (1 - c) + chip)

    @pl.when(not_last)
    def _():
        await_into(xa.at[1 - c, :, 3], up_sib)

    @pl.when(not_first)
    def _():
        await_into(xa.at[1 - c, :, 0], down_sib)

    for i in range(4):
        first = xa[0, i].astype(F32).reshape(256, 128)
        second = xa[1, i].astype(F32).reshape(256, 128)
        xn[0, :, :, :, 128 * i:128 * i + 128] = (
            merge(first, second).astype(BF).reshape(4, 4, 16, 128))
        xn[1, :, :, :, 128 * i:128 * i + 128] = (
            merge_high(first, second).astype(BF).reshape(4, 4, 16, 128))

    copies[4].wait()
    for a, b in TAPS:
        n = 2 + a
        left = xn[:, b:b + 2, 0:n].reshape(64 * n, 512)
        tap = 3 * (3 * a + b)
        right = w1[tap:tap + 3].reshape(192, 512)
        v = dot(left, right, ((1,), (1,))).reshape(2, 2, n, 16, 192)
        acc[:, :, 2 - a:4, :, 0:192] = acc[:, :, 2 - a:4, :, 0:192] + v
    low0 = acc[0, :, :, :, 0:128].reshape(128, 128)
    low1 = acc[0, :, :, :, 128:256].reshape(128, 128)
    high0 = acc[1, :, :, :, 0:128].reshape(128, 128)
    high1 = acc[1, :, :, :, 128:256].reshape(128, 128)
    wide_bias = jnp.concatenate([bias[...], bias[...]], axis=1)
    preact = (prev_column(merge(low0, high0)) + merge_high(low0, high0)
              + next_column(merge(low1, high1)) + wide_bias)
    act_two = silu(preact).astype(BF).astype(F32)

    xs2[...] = transposed(act_two)
    x2_cross = reserve("recv", 1)
    x2_base = reserve("recv", 32)
    post(xs2, xr2, x2_cross, (d, partner, t), jnp.logical_not(home))

    def distribute(src, half):
        for i in (0, 1, 3, 2):
            for j in (2, 1, 3, 0):
                if i or j:
                    other, chip = (x + i) % NX, (k + j) % 4
                    post(src.at[other], xt2.at[half, x, k],
                         x2_base + 16 * half + 4 * x + k,
                         (d, z * NX + other, 2 * chip + c), home)

        @pl.when(home)
        def _():
            xt2[half, x, k] = src[x]

    distribute(xs2, z)
    far_relay(gc, c_base)

    grad_pre = scatter_end(e_base, e2r).reshape(128, 128) * slope(preact)
    grad_rows = grad_pre.astype(BF).reshape(2, 4, 16, 128)
    gn[1:3] = grad_rows
    gp[pl.ds(2 * h, 2)] = grad_rows
    gn_base = near_begin(gn)
    p_base = far_begin(gp)

    @pl.when(home)
    def _():
        await_into(xr2, x2_cross)

    distribute(xr2, 1 - z)

    x1_sib = reserve("recv", 8)
    for i in (z, 1 - z):
        for j in range(NX):
            other = (x + j) % NX
            block = xt1.at[i, other]
            source = i * NX + other

            @pl.when(home if j else home & (i != z))
            def _():
                await_into(block, x1_base + source)

            post(block, block, x1_sib + source, sibling, home)

    far_end(gc, c_base)
    spread(gc, g3c, 1)

    near_end(gn, gn_base)
    spread(gn, g3n, 0)
    transposed_conv(w1)
    h_base = scatter_begin(h1, h1r)
    far_relay(gp, p_base)

    x2_sib = reserve("recv", 8)
    for half in (z, 1 - z):
        for i in range(NX):
            other = (x + i) % NX

            @pl.when(home)
            def _():
                for j in range(4):
                    chip = (k + j) % 4
                    if i or j:
                        await_into(xt2.at[half, other, chip],
                                   x2_base + 16 * half + 4 * other + chip)

            post(xt2.at[half, other], xt2.at[half, other],
                 x2_sib + NX * half + other, sibling, home)

    h_base = scatter_on(h_base, h1r, h2, h2r)

    def await_sibling(xt, base):
        @pl.when(jnp.logical_not(home))
        def _():
            for i in range(NX * NZ):
                await_into(xt.at[i // NX, i % NX], base + i)

    await_sibling(xt2, x2_sib)
    y2_base = grad_begin(xt2, g3c, sf2, sy2, ry2)
    far_end(gp, p_base)
    spread(gp, g3p, 1)
    await_sibling(xt1, x1_sib)
    y1_base = grad_begin(xt1, g3p, sf1, sy1, ry1)

    back = scatter_end(h_base, h2r)
    grad_in = cotp[...] + back * slope(featp[...])
    for r in range(2):
        for f in range(4):
            out_in[0, f, r, 0:16] = grad_in[r, f, :, 0:64].astype(BF)
            out_in[0, f, r, 16:32] = grad_in[r, f, :, 64:128].astype(BF)
    results = [
        pltpu.make_async_copy(src, dst, out_sem.at[i]) for i, (src, dst) in enumerate(
            [(out_in, in_hbm), (out_two, two_hbm), (out_one, one_hbm)])
    ]
    results[0].start()
    grad_end(y2_base, sf2, ry2, out_two)
    results[1].start()
    grad_end(y1_base, sf1, ry1, out_one)
    results[2].start()

    for finish, when in unfinished:
        if when is None:
            finish()
        else:
            pl.when(when)(finish)
    for copy in results:
        copy.wait()
    assert counts["send"] <= SENDS and counts["recv"] <= RECVS


def write_kernel(a, b, c, a_out, b_out, c_out, a_mid, b_mid, c_mid, in_sem, out_sem):
    stages = [(a, a_mid, a_out), (b, b_mid, b_out), (c, c_mid, c_out)]
    first = [
        pltpu.make_async_copy(src, mid, in_sem.at[i])
        for i, (src, mid, _) in enumerate(stages)
    ]
    second = [
        pltpu.make_async_copy(mid, dst, out_sem.at[i])
        for i, (_, mid, dst) in enumerate(stages)
    ]
    for copy in first:
        copy.start()
    for copy, after in zip(first, second):
        copy.wait()
        after.start()
    for copy in second:
        copy.wait()


def local(features, cotangent, conv_one, bias_one, conv_two):
    hbm = pl.BlockSpec(memory_space=pltpu.HBM)
    grad_in_shape = (1, 4, 2, 32, 64)
    block = (2, 4, 16, 128)
    blocks = pltpu.VMEM((4,) + block, BF)
    near = pltpu.VMEM((4, 4, 16, 128), BF)
    far = pltpu.VMEM((16, 4, 16, 128), BF)
    wide = pltpu.VMEM((2, 18, 6, 16, 256), BF)
    turned = pltpu.VMEM((4, 16, 256), BF)
    clip = pltpu.VMEM((2, 4, 4, 16, 256), BF)
    sums = pltpu.VMEM((4, 3, 5, 16, 128), F32)
    sent = pltpu.VMEM((4, 3, 5, 16, 128), BF)
    kernel_block = pltpu.VMEM((27, 64, 512), BF)
    scratch = [
        pltpu.VMEM(grad_in_shape, BF), pltpu.VMEM(grad_in_shape, BF),
        pltpu.VMEM((1, 64), F32), kernel_block, kernel_block,
        pltpu.VMEM((2, 4, 4, 4, 16, 128), BF), pltpu.VMEM((2, 4, 4, 16, 512), BF),
        near, near, far, far, pltpu.VMEM((2, 4, 4, 16, 256), BF), wide, wide,
        pltpu.VMEM((2, 2, 4, 16, 512), F32), pltpu.VMEM((2, 2, 4, 16, 256), F32),
        pltpu.VMEM((4,) + block, F32),
        blocks, blocks, blocks, blocks, blocks, blocks, blocks, blocks,
        pltpu.VMEM((4, 4, 16, 256), BF), turned, turned, clip, clip,
        sums, sums, sent, sent, sent, sent,
        pltpu.VMEM(block, F32), pltpu.VMEM(block, F32),
        pltpu.VMEM(grad_in_shape, BF),
        pltpu.VMEM((27, 16, 64), F32), pltpu.VMEM((27, 16, 64), F32),
        pltpu.SemaphoreType.DMA((5,)), pltpu.SemaphoreType.DMA((3,)),
        pltpu.SemaphoreType.DMA((SENDS,)), pltpu.SemaphoreType.DMA((RECVS,)),
    ]
    out_shape = (
        jax.ShapeDtypeStruct(grad_in_shape, BF),
        jax.ShapeDtypeStruct((27, 16, 64), F32),
        jax.ShapeDtypeStruct((27, 16, 64), F32),
    )
    outs = pl.pallas_call(
        kernel,
        out_shape=out_shape,
        in_specs=[hbm, hbm, hbm, hbm, hbm],
        out_specs=(hbm, hbm, hbm),
        scratch_shapes=scratch,
        compiler_params=pltpu.CompilerParams(
            collective_id=0, has_side_effects=True, vmem_limit_bytes=56 * 1024 * 1024
        ),
    )(features, cotangent, bias_one.reshape(1, -1), conv_one, conv_two)
    return pl.pallas_call(
        write_kernel,
        out_shape=out_shape,
        in_specs=[hbm, hbm, hbm],
        out_specs=(hbm, hbm, hbm),
        scratch_shapes=[
            pltpu.VMEM(grad_in_shape, BF),
            pltpu.VMEM((27, 16, 64), F32), pltpu.VMEM((27, 16, 64), F32),
            pltpu.SemaphoreType.DMA((3,)), pltpu.SemaphoreType.DMA((3,)),
        ],
        compiler_params=pltpu.CompilerParams(vmem_limit_bytes=60 * 1024 * 1024),
    )(*outs)


def solution(mesh):
    in_specs = (
        P("dp", None, "height", None, "tensor"),
        P("dp", None, "height", None, "tensor"),
        P(None, "tensor", None),
        P("tensor"),
        P(None, "tensor", None),
    )
    out_specs = (
        P("dp", None, "height", None, "tensor"),
        P(None, ("dp", "height"), "tensor"),
        P(None, ("dp", "height"), "tensor"),
    )
    return jax.shard_map(local, mesh=mesh, in_specs=in_specs, out_specs=out_specs, check_vma=False)
```

time: 758 us -> 52.3 us (0.07); the launches traced: 743 us -> 51.4 us
  waiting for transfers between devices: 417 us -> 0 us
  local copies, waits for them, and re-layouts: 210 us -> 0 us
  Pallas kernels: 0 us -> 50.7 us
  blocking collectives: 35.1 us -> 0 us
  starting transfers between devices: 26.5 us -> 0 us
  matrix products: 25.3 us -> 0 us
  other arithmetic: 14.5 us -> 0 us
  between operations: 14.5 us -> 0.64 us
    reduce_scatter x2 -> x0, waiting for transfers between devices: 399 us -> none  [the longest x1 260 us: settle_grads(): lax.psum_scatter(terms[0], ('dp', 'height'), scatter_dimension=1, tiled=T...]
    unnamed x140 -> x0, local copies, waits for them, and re-layouts: 125 us -> none
    another operation x11 -> x0, local copies, waits for them, and re-layouts: 59.6 us -> none  [the longest x5 48.1 us: forward_patches(): stacked = jnp.stack(windows, axis=-2)]
    pallas_call x0 -> x2, Pallas kernels: none -> 50.7 us  [the longest x1 48.9 us: local(): pl.pallas_call(kernel, out_shape=out_shape, in_specs=[hbm, hbm, hbm, hbm,...]
    all_gather x2 -> x0, blocking collectives: 35.1 us -> none  [widen(): return lax.all_gather(value, 'tensor', axis=4, tiled=True)]
    ppermute x8 -> x0, starting transfers between devices: 26 us -> none  [the longest x4 16.3 us: with_halo(): before = lax.ppermute(last, axis, up)]
    dot_general x5 -> x0, matrix products: 25.3 us -> none  [the longest x2 16 us: contract_rows(): lax.dot_general(left, right, (((0,), (0,)), ((), ())), preferred_element_...]
    dot_general x2 -> x0, local copies, waits for them, and re-layouts: 20.6 us -> none  [contract_rows(): lax.dot_general(left, right, (((0,), (0,)), ((), ())), preferred_element_...]
  transfers between devices with their start and end apart: 12 -> 0, of which waited for: 5 -> 0; matrix products, arithmetic and copies ran while one was open for 30% -> 0% of each run, Pallas kernels for 0% -> 0%
where the time goes in v2:
time: 52.3 us; the launch traced here: 51.4 us
  Pallas kernels  50.7 us (97%)
  between operations  0.64 us (1%)
    pallas_call x1, Pallas kernels, local(): pl.pallas_call(kernel, out_shape=out_shape, in_specs=[hbm, hbm, hbm, hbm,...  48.9 us
    pallas_call x1, Pallas kernels, local(): pl.pallas_call(write_kernel, out_shape=out_shape, in_specs=[hbm, hbm, hbm...  1.82 us

profile of v2, /device:TPU:2, one launch (start us, length us, event | category | flops | bytes accessed | tf_op | source)
XLA Modules:
  0.0 51.4 jit_solution(14215461224768010751)
XLA Ops:
  0.6 48.9 %shard_map.76 = (bf16[1,4,2,32,64]{4,3,2,1,0:T(8,128)(2,1)}, f32[27,16,64]{2,1,0:T(8,128)}, f32[27,16,64]{2,1,0:T(8,128)}) custom-call(bf16[1,4,2,32,64]{4,3,2,1,0:T(8,128)(2,1)} %feat_hbm.1, bf16[1,4,2,32,64]{4,3,2,1,0:T(8,128)(2,1)} %cot_hbm.1, f32[1,64]{1,0:T(1,128)} %bitcast.1, bf16[27,64,512]{2,1,0:T(8,128)(2,1)} %w1_hbm.1, bf16[27,64,512]{2,1,0:T(8,128)(2,1)} %w2_hbm.1), custom_call_target="tpu_custom_call" | custom-call | tf_op jit(solution)/shard_map/pallas_call | solution.py:606
  49.5 1.8 %shard_map.77 = (bf16[1,4,2,32,64]{4,3,2,1,0:T(8,128)(2,1)}, f32[27,16,64]{2,1,0:T(8,128)}, f32[27,16,64]{2,1,0:T(8,128)}) custom-call(bf16[1,4,2,32,64]{4,3,2,1,0:T(8,128)(2,1)} %get-tuple-element.6.a, f32[27,16,64]{2,1,0:T(8,128)} %get-tuple-element.7.b, f32[27,16,64]{2,1,0:T(8,128)} %get-tuple-element.8.c), custom_call_target="tpu_custom_call" | custom-call | tf_op jit(solution)/shard_map/pallas_call | solution.py:616

commit v3 on v2

--- a/solution.py
+++ b/solution.py
@@ -121,6 +121,14 @@
             pl.when(when)(begin)
         unfinished.append((finish, when))
 
+    def finish_all():
+        for finish, when in unfinished:
+            if when is None:
+                finish()
+            else:
+                pl.when(when)(finish)
+        unfinished.clear()
+
     def await_into(dst, r):
         remote(dst, dst, 0, r, here).wait_recv()
 
@@ -283,7 +291,7 @@
         v = jnp.transpose(packed)
         return jnp.concatenate([v[:64], v[64:]], axis=1).astype(BF).reshape(4, 16, 256)
 
-    def grad_begin(xt, g3, sf, sy, ry):
+    def grad_begin(xt, g3, sf, sy, ry, parts):
         base = reserve("recv", 12)
         for a in range(3):
             sides = []
@@ -302,27 +310,32 @@
                 tile = v.reshape(4, 16, 128)
                 sf[:, a, i] = tile
                 sy[:, a, i] = tile.astype(BF)
-            for j in (2, 1, 3):
-                other = (d + j) % NY
-                post(sy.at[other, a], ry.at[d, a], base + 4 * a + d, (other, h, t))
+            for first, n in parts:
+                if first + n - 1 == a:
+                    piece = pl.ds(first, n)
+                    for j in (2, 1, 3):
+                        other = (d + j) % NY
+                        post(sy.at[other, piece], ry.at[d, piece], base + 4 * first + d,
+                             (other, h, t))
         return base
 
     scale = 1.0 / math.sqrt(4 * 4 * 16 * 32)
 
-    def grad_end(base, sf, ry, out):
-        for a in range(3):
-            v = sf[d, a]
+    def grad_end(base, sf, ry, out, parts):
+        for first, n in parts:
+            v = sf[d, first:first + n]
             for j in range(1, NY):
                 other = (d + j) % NY
-                await_into(ry.at[other, a], base + 4 * a + other)
-                v = v + ry[other, a].astype(F32)
+                await_into(ry.at[other, pl.ds(first, n)], base + 4 * first + other)
+                v = v + ry[other, first:first + n].astype(F32)
             v = v * scale
-            for b in range(3):
-                tap = 9 * a + 3 * b
-                out[tap] = v[b, :, 0:64]
-                out[tap + 1] = v[b, :, 64:128]
-                side = v[3 + b // 2]
-                out[tap + 2] = side[:, 64:128] if b == 1 else side[:, 0:64]
+            for a in range(n):
+                for b in range(3):
+                    tap = 9 * (first + a) + 3 * b
+                    out[tap] = v[a, b, :, 0:64]
+                    out[tap + 1] = v[a, b, :, 64:128]
+                    side = v[a, 3 + b // 2]
+                    out[tap + 2] = side[:, 64:128] if b == 1 else side[:, 0:64]
 
     a_base = reserve("recv", 8)
     up_base = reserve("recv", 8)
@@ -369,10 +382,6 @@
     for i in range(4):
         xs1[:, i] = transposed(xa[c, i, 1:3].astype(F32).reshape(128, 128))
     x1_base = reserve("recv", 8)
-    for j in (2, 1, 3, 0):
-        other = (x + j) % NX
-        post(xs1.at[other], xt1.at[z, x], x1_base + h, (d, c * NX + other, t),
-             None if j else jnp.logical_not(home))
 
     @pl.when(home)
     def _():
@@ -456,6 +465,10 @@
             xt2[half, x, k] = src[x]
 
     distribute(xs2, z)
+    for j in (2, 1, 3, 0):
+        other = (x + j) % NX
+        post(xs1.at[other], xt1.at[z, x], x1_base + h, (d, c * NX + other, t),
+             None if j else jnp.logical_not(home))
     far_relay(gc, c_base)
 
     grad_pre = scatter_end(e_base, e2r).reshape(128, 128) * slope(preact)
@@ -482,7 +495,7 @@
             def _():
                 await_into(block, x1_base + source)
 
-            post(block, block, x1_sib + source, sibling, home)
+        post(xt1.at[i], xt1.at[i], x1_sib + i, sibling, home)
 
     far_end(gc, c_base)
     spread(gc, g3c, 1)
@@ -506,23 +519,24 @@
                         await_into(xt2.at[half, other, chip],
                                    x2_base + 16 * half + 4 * other + chip)
 
-            post(xt2.at[half, other], xt2.at[half, other],
-                 x2_sib + NX * half + other, sibling, home)
+        post(xt2.at[half], xt2.at[half], x2_sib + half, sibling, home)
 
     h_base = scatter_on(h_base, h1r, h2, h2r)
 
     def await_sibling(xt, base):
         @pl.when(jnp.logical_not(home))
         def _():
-            for i in range(NX * NZ):
-                await_into(xt.at[i // NX, i % NX], base + i)
-
+            for i in range(NZ):
+                await_into(xt.at[i], base + i)
+
+    whole, cut = ((0, 3),), ((0, 1), (1, 1), (2, 1))
     await_sibling(xt2, x2_sib)
-    y2_base = grad_begin(xt2, g3c, sf2, sy2, ry2)
+    y2_base = grad_begin(xt2, g3c, sf2, sy2, ry2, whole)
     far_end(gp, p_base)
     spread(gp, g3p, 1)
     await_sibling(xt1, x1_sib)
-    y1_base = grad_begin(xt1, g3p, sf1, sy1, ry1)
+    y1_base = grad_begin(xt1, g3p, sf1, sy1, ry1, cut)
+    finish_all()
 
     back = scatter_end(h_base, h2r)
     grad_in = cotp[...] + back * slope(featp[...])
@@ -535,16 +549,12 @@
             [(out_in, in_hbm), (out_two, two_hbm), (out_one, one_hbm)])
     ]
     results[0].start()
-    grad_end(y2_base, sf2, ry2, out_two)
+    grad_end(y2_base, sf2, ry2, out_two, whole)
     results[1].start()
-    grad_end(y1_base, sf1, ry1, out_one)
+    grad_end(y1_base, sf1, ry1, out_one, cut)
     results[2].start()
 
-    for finish, when in unfinished:
-        if when is None:
-            finish()
-        else:
-            pl.when(when)(finish)
+    finish_all()
     for copy in results:
         copy.wait()
     assert counts["send"] <= SENDS and counts["recv"] <= RECVS

time: 52.3 us -> 51.3 us (0.981); the launches traced: 51.4 us -> 51.2 us
  no operation moved by 1% of the time
where the time goes in v3:
time: 51.3 us; the launch traced here: 51.2 us
  Pallas kernels  50.6 us (99%)
  between operations  0.64 us (1%)
    pallas_call x1, Pallas kernels, local(): pl.pallas_call(kernel, out_shape=out_shape, in_specs=[hbm, hbm, hbm, hbm,...  48.8 us
    pallas_call x1, Pallas kernels, local(): pl.pallas_call(write_kernel, out_shape=out_shape, in_specs=[hbm, hbm, hbm...  1.82 us

profile of v3, /device:TPU:2, one launch (start us, length us, event | category | flops | bytes accessed | tf_op | source)
XLA Modules:
  0.0 51.2 jit_solution(10720634892603223329)
XLA Ops:
  0.6 48.8 %shard_map.76 = (bf16[1,4,2,32,64]{4,3,2,1,0:T(8,128)(2,1)}, f32[27,16,64]{2,1,0:T(8,128)}, f32[27,16,64]{2,1,0:T(8,128)}) custom-call(bf16[1,4,2,32,64]{4,3,2,1,0:T(8,128)(2,1)} %feat_hbm.1, bf16[1,4,2,32,64]{4,3,2,1,0:T(8,128)(2,1)} %cot_hbm.1, f32[1,64]{1,0:T(1,128)} %bitcast.1, bf16[27,64,512]{2,1,0:T(8,128)(2,1)} %w1_hbm.1, bf16[27,64,512]{2,1,0:T(8,128)(2,1)} %w2_hbm.1), custom_call_target="tpu_custom_call" | custom-call | tf_op jit(solution)/shard_map/pallas_call | solution.py:616
  49.4 1.8 %shard_map.77 = (bf16[1,4,2,32,64]{4,3,2,1,0:T(8,128)(2,1)}, f32[27,16,64]{2,1,0:T(8,128)}, f32[27,16,64]{2,1,0:T(8,128)}) custom-call(bf16[1,4,2,32,64]{4,3,2,1,0:T(8,128)(2,1)} %get-tuple-element.6.a, f32[27,16,64]{2,1,0:T(8,128)} %get-tuple-element.7.b, f32[27,16,64]{2,1,0:T(8,128)} %get-tuple-element.8.c), custom_call_target="tpu_custom_call" | custom-call | tf_op jit(solution)/shard_map/pallas_call | solution.py:626

commit v4 on v3

--- a/solution.py
+++ b/solution.py
@@ -561,7 +561,12 @@
 
 
 def write_kernel(a, b, c, a_out, b_out, c_out, a_mid, b_mid, c_mid, in_sem, out_sem):
-    stages = [(a, a_mid, a_out), (b, b_mid, b_out), (c, c_mid, c_out)]
+    stages = []
+    for first in range(0, 27, 9):
+        part = pl.ds(first, 9)
+        stages.append((c.at[part], c_mid.at[part], c_out.at[part]))
+        stages.append((b.at[part], b_mid.at[part], b_out.at[part]))
+    stages.append((a, a_mid, a_out))
     first = [
         pltpu.make_async_copy(src, mid, in_sem.at[i])
         for i, (src, mid, _) in enumerate(stages)
@@ -631,7 +636,7 @@
         scratch_shapes=[
             pltpu.VMEM(grad_in_shape, BF),
             pltpu.VMEM((27, 16, 64), F32), pltpu.VMEM((27, 16, 64), F32),
-            pltpu.SemaphoreType.DMA((3,)), pltpu.SemaphoreType.DMA((3,)),
+            pltpu.SemaphoreType.DMA((7,)), pltpu.SemaphoreType.DMA((7,)),
         ],
         compiler_params=pltpu.CompilerParams(vmem_limit_bytes=60 * 1024 * 1024),
     )(*outs)

time: 51.3 us -> 51.4 us (level)
  no operation moved by 1% of the time
where the time goes in v4:
time: 51.4 us; the launch traced here: 51.3 us
  Pallas kernels  50.6 us (98%)
  between operations  0.64 us (1%)
    pallas_call x1, Pallas kernels, local(): pl.pallas_call(kernel, out_shape=out_shape, in_specs=[hbm, hbm, hbm, hbm,...  48.8 us
    pallas_call x1, Pallas kernels, local(): pl.pallas_call(write_kernel, out_shape=out_shape, in_specs=[hbm, hbm, hbm...  1.84 us

profile of v4, /device:TPU:2, one launch (start us, length us, event | category | flops | bytes accessed | tf_op | source)
XLA Modules:
  0.0 51.3 jit_solution(17951476604726555831)
XLA Ops:
  0.6 48.8 %shard_map.76 = (bf16[1,4,2,32,64]{4,3,2,1,0:T(8,128)(2,1)}, f32[27,16,64]{2,1,0:T(8,128)}, f32[27,16,64]{2,1,0:T(8,128)}) custom-call(bf16[1,4,2,32,64]{4,3,2,1,0:T(8,128)(2,1)} %feat_hbm.1, bf16[1,4,2,32,64]{4,3,2,1,0:T(8,128)(2,1)} %cot_hbm.1, f32[1,64]{1,0:T(1,128)} %bitcast.1, bf16[27,64,512]{2,1,0:T(8,128)(2,1)} %w1_hbm.1, bf16[27,64,512]{2,1,0:T(8,128)(2,1)} %w2_hbm.1), custom_call_target="tpu_custom_call" | custom-call | tf_op jit(solution)/shard_map/pallas_call | solution.py:621
  49.4 1.8 %shard_map.77 = (bf16[1,4,2,32,64]{4,3,2,1,0:T(8,128)(2,1)}, f32[27,16,64]{2,1,0:T(8,128)}, f32[27,16,64]{2,1,0:T(8,128)}) custom-call(bf16[1,4,2,32,64]{4,3,2,1,0:T(8,128)(2,1)} %get-tuple-element.6.a, f32[27,16,64]{2,1,0:T(8,128)} %get-tuple-element.7.b, f32[27,16,64]{2,1,0:T(8,128)} %get-tuple-element.8.c), custom_call_target="tpu_custom_call" | custom-call | tf_op jit(solution)/shard_map/pallas_call | solution.py:631
